TPU v7x, 512 devices: a whole 4x8x8 slice. The times are simulated.
512 devices in a mesh: rep: 32 (over y, z_lo, core), fsdp: 16 (over z_hi, x).
Axes of the slice: x: 4, y: 8, z: 8 (z_hi: 4, z_lo: 2; z = z_hi * 2 + z_lo), core: 2. Of those that a mesh axis runs over, the one named last changes fastest.
Arguments:
- tokens: bfloat16 [16384, 4096], P('rep', 'fsdp'), may hold values from -6 to 6
- gate_weight: bfloat16 [4096, 7168], P('rep', 'fsdp'), may hold values from -0.09375 to 0.09375
- up_act: bfloat16 [16384, 7168], P('rep', 'fsdp'), may hold values from -6 to 6
- cotangent: bfloat16 [16384, 7168], P('rep', 'fsdp'), may hold values from -0.099609375 to 0.099609375
Outputs:
- grad_sum: bfloat16 [4096, 7168], P('rep', 'fsdp')
- curvature: float32 [7168], P('fsdp')
- spread: float32 [7168], P('fsdp')
All inputs are finite; a program needn't handle non-finite values.
Results may differ from a plain program's by a relative error of at most 0.024.
Values may be sent and summed in bfloat16 or wider, within the bound.
No kernel may reach another device: no remote copies, remote signals or barrier semaphores. Data moves between devices by JAX's collectives and lax.ppermute only.
A program may use at most 64 MiB of HBM per device.

v0:
```python
import jax
import jax.numpy as jnp
from jax import lax
from jax.sharding import Mesh
from jax.sharding import PartitionSpec as P

REP = ("rep_0", "rep_1", "rep_2")


def copy_for_each(value, axis):
    count = lax.axis_size(axis)
    return lax.all_to_all(
        jnp.broadcast_to(value[None], (count, *value.shape)), axis, 0, 0, tiled=True
    )


def in_order(blocks, dim):
    blocks = jnp.moveaxis(blocks, 0, dim)
    lengths = blocks.shape
    return blocks.reshape(*lengths[:dim], lengths[dim] * lengths[dim + 1], *lengths[dim + 2 :])


def gathered_by_axis(value, axes, dim):
    far, near = axes
    blocks = copy_for_each(copy_for_each(value, far), near)
    return in_order(blocks.swapaxes(0, 1).reshape(-1, *value.shape), dim)


def padded_to(lines, count):
    spare = -len(lines) % count
    return jnp.pad(lines, [(0, spare)] + [(0, 0)] * (lines.ndim - 1))


def in_blocks(value, dim, count):
    lengths = value.shape
    blocks = value.reshape(*lengths[:dim], count, lengths[dim] // count, *lengths[dim + 1 :])
    return jnp.moveaxis(blocks, dim, 0)


def summed_on_arrival(value, axis, dim):
    count = lax.axis_size(axis)
    blocks = lax.all_to_all(in_blocks(value, dim, count), axis, 0, 0, tiled=True)
    return jnp.sum(blocks.astype(jnp.float32), axis=0)


def sum_in_two_steps(value, axes, dim):
    far, near = axes
    own = summed_on_arrival(in_blocks(value, dim, lax.axis_size(far)), near, dim + 1)
    return jnp.sum(
        lax.all_to_all(own.astype(jnp.bfloat16), far, 0, 0, tiled=True).astype(jnp.float32), axis=0
    )


def total_of(value, axes):
    lines = value.reshape(-1, value.shape[-1])
    padded = padded_to(lines, lax.axis_size(axes[0]) * lax.axis_size(axes[1]))
    whole = gathered_by_axis(sum_in_two_steps(padded, axes, 0).astype(jnp.bfloat16), axes, 0)
    return lax.slice_in_dim(whole, 0, len(lines)).reshape(value.shape).astype(jnp.float32)


def over_copies(value, axis):
    everything = copy_for_each(value, axis)
    return jnp.sum(everything, axis=0)


def in_one(arrays, axis):
    ravelled, at, outs = (jnp.concatenate([a.reshape(-1) for a in arrays]), 0, [])
    running = over_copies(ravelled, axis)
    for a in arrays:
        outs.append(running[at : at + a.size].reshape(a.shape))
        at += a.size
    return tuple(outs)


def shards(tokens, gate_weight, up_act, cotangent):
    features_all = lax.all_gather(tokens, "fsdp", axis=1, tiled=True)
    replicas = lax.axis_size(REP)
    gate_pre = jnp.dot(
        features_all,
        gathered_by_axis(gate_weight, (("rep_0", "rep_1"), "rep_2"), 0),
        preferred_element_type=jnp.float32,
    )
    sigmoid_gate = jax.nn.sigmoid(gate_pre)
    deriv_one = sigmoid_gate * (1.0 + gate_pre * (1.0 - sigmoid_gate))
    deriv_two = sigmoid_gate * (1.0 - sigmoid_gate) * (2.0 + gate_pre * (1.0 - 2.0 * sigmoid_gate))
    weighted = cotangent.astype(jnp.float32) * up_act.astype(jnp.float32)
    token_coeff = (weighted * deriv_one).astype(jnp.bfloat16)
    bend_weight = weighted * deriv_two
    rep_grad = lax.dot_general(
        features_all, token_coeff, (((0,), (0,)), ((), ())), preferred_element_type=jnp.float32
    ).astype(jnp.bfloat16)
    own_proj = jnp.dot(features_all, rep_grad, preferred_element_type=jnp.float32)
    grad_full = total_of(
        rep_grad.astype(jnp.float32).astype(jnp.bfloat16), (("rep_0", "rep_1"), "rep_2")
    ).astype(jnp.bfloat16)
    shard_rows = grad_full.shape[0] // replicas
    grad_shard = lax.dynamic_slice_in_dim(
        grad_full, lax.axis_index(REP) * shard_rows, shard_rows, 0
    )
    mean_proj = jnp.dot(features_all, grad_full, preferred_element_type=jnp.float32) / replicas
    deviate = own_proj - mean_proj
    curv_part = jnp.sum(bend_weight * mean_proj * mean_proj, axis=0)
    spread_part = jnp.sum(bend_weight * deviate * deviate, axis=0)
    curvature, spread_total = in_one((curv_part, spread_part), REP)
    return (grad_shard, curvature, spread_total / (replicas - 1))


def solution(mesh):
    torus = Mesh(
        mesh.devices.reshape(8, 2, 2, mesh.shape["fsdp"]), ("rep_0", "rep_1", "rep_2", "fsdp")
    )
    in_specs = (P(REP, "fsdp"), P(REP, "fsdp"), P(REP, "fsdp"), P(REP, "fsdp"))
    out_specs = (P(REP, "fsdp"), P("fsdp"), P("fsdp"))
    return jax.shard_map(
        shards, mesh=torus, in_specs=in_specs, out_specs=out_specs, check_vma=False
    )
```

profile of v0, /device:TPU:1, one launch (start us, length us, event | category | flops | bytes accessed | tf_op | source)
XLA Modules:
  0.0 298.9 jit_solution(17605486827183492126)
XLA Ops:
  7.2 0.7 all-gather.2.cloned.1.call-update
  7.9 1.2 broadcast_in_dim.10
  9.2 53.8 %all_to_all.36 = bf16[16,128,448]{1,2,0:T(8,128)(2,1)S(1)} all-to-all(bf16[16,128,448]{1,2,0:T(8,128)(2,1)S(1)} %broadcast_in_dim.10), channel_id=1, replica_groups=mesh['rep_0'=8,'rep_1'=2,'rep_2'=2,'fsdp'=16] {'rep_0','rep_1'}, dimensions={0} | all-to-all | bytes 3670016 | tf_op jit(solution)/shard_map/all_to_all | solution.py:12
  63.0 1.2 copy.28
  64.1 0.5 broadcast_in_dim.11
  64.6 8.7 %all_to_all.37 = bf16[2,16,128,448]{2,1,3,0:T(8,128)(2,1)S(1)} all-to-all(bf16[2,16,128,448]{2,1,3,0:T(8,128)(2,1)S(1)} %broadcast_in_dim.11), channel_id=1, replica_groups=mesh['rep_0'=8,'rep_1'=2,'rep_2'=2,'fsdp'=16] {'rep_2'}, dimensions={0} | all-to-all | bytes 7340032 | tf_op jit(solution)/shard_map/all_to_all | solution.py:12
  73.3 7.5 %copy.29 = bf16[16,2,128,448]{2,1,0,3:T(2,128)(2,1)} copy(bf16[16,2,128,448]{2,0,3,1:T(8,128)(2,1)S(1)} %bitcast.29) | data formatting | bytes 7340032 | tf_op jit(solution)/shard_map/transpose | solution.py:26
  80.8 7.2 %reshape_reshape.9 = bf16[4096,448]{0,1:T(8,128)(2,1)} reshape(bf16[16,2,128,448]{2,1,0,3:T(2,128)(2,1)} %copy.29) | data formatting | bytes 7340032 | tf_op jit(solution)/shard_map/reshape;reshape | solution.py:20
  88.0 24.2 %all-gather.2.cloned.1.call-done = bf16[512,4096]{1,0:T(8,128)(2,1)} async-done(((bf16[512,256]{1,0:T(8,128)(2,1)}), bf16[512,4096]{1,0:T(8,128)(2,1)}) %all-gather.2.cloned.1.call-update) | async-done | bytes 4194320 | tf_op jit(solution)/shard_map/all_gather | solution.py:76
  112.2 5.5 %fusion.13 = f32[512,448]{0,1:T(8,128)S(1)} fusion(bf16[512,4096]{1,0:T(8,128)(2,1)} %all-gather.2.cloned.1.call-done, bf16[4096,448]{0,1:T(8,128)(2,1)} %reshape_reshape.9), kind=kOutput, calls=%fused_computation.25 | convolution fusion | flops 1879048192 | bytes 8781824 | tf_op jit(solution)/shard_map/dot_general | solution.py:78
  117.8 4.1 %convolution_convert_fusion = bf16[448,4096]{1,0:T(8,128)(2,1)} fusion(bf16[512,4096]{1,0:T(8,128)(2,1)S(1)} %copy-done.1, f32[512,448]{0,1:T(8,128)S(1)} %fusion.13, bf16[512,448]{0,1:T(8,128)(2,1)S(1)} %copy-done.3, bf16[512,448]{0,1:T(8,128)(2,1)S(1)} %copy-done.4), kind=kOutput, calls=%fused_computation | convolution fusion | flops 1883635712 | bytes 9699328 | tf_op jit(solution)/shard_map/dot_general | solution.py:89
  121.9 7.1 %reshape_reshape.10 = bf16[16,2,128,448]{2,1,0,3:T(2,128)(2,1)} reshape(bf16[4096,448]{0,1:T(8,128)(2,1)} %bitcast.32) | data formatting | bytes 7340032 | tf_op jit(solution)/shard_map/reshape;reshape | solution.py:36
  129.0 2.5 copy.41
  131.5 7.9 %all_to_all.38 = bf16[2,16,128,448]{2,1,3,0:T(8,128)(2,1)} all-to-all(bf16[2,16,128,448]{2,1,3,0:T(8,128)(2,1)S(1)} %bitcast.30), channel_id=1, replica_groups=mesh['rep_0'=8,'rep_1'=2,'rep_2'=2,'fsdp'=16] {'rep_2'}, dimensions={0} | all-to-all | bytes 7340032 | tf_op jit(solution)/shard_map/all_to_all | solution.py:42
  139.5 4.0 %reduce_sum.51 = bf16[16,128,448]{1,0,2:T(8,128)(2,1)S(1)} reduce(bf16[2,16,128,448]{2,1,3,0:T(8,128)(2,1)} %all_to_all.38, bf16[]{:T(256)} %constant.11.clone.1), dimensions={0}, to_apply=%region_0.1 | reduce | flops 917504 | bytes 5505026 | tf_op jit(solution)/shard_map/reduce_sum | solution.py:43
  143.4 0.5 copy.32
  143.9 51.3 %all_to_all.39 = bf16[16,128,448]{1,2,0:T(8,128)(2,1)S(1)} all-to-all(bf16[16,128,448]{1,2,0:T(8,128)(2,1)S(1)} %copy.32), channel_id=1, replica_groups=mesh['rep_0'=8,'rep_1'=2,'rep_2'=2,'fsdp'=16] {'rep_0','rep_1'}, dimensions={0} | all-to-all | bytes 3670016 | tf_op jit(solution)/shard_map/all_to_all | solution.py:50
  195.2 0.3 reduce_sum.52
  195.5 0.3 broadcast_in_dim.12
  195.8 47.7 %all_to_all.40 = bf16[16,128,448]{1,2,0:T(8,128)(2,1)S(1)} all-to-all(bf16[16,128,448]{1,2,0:T(8,128)(2,1)S(1)} %broadcast_in_dim.12), channel_id=1, replica_groups=mesh['rep_0'=8,'rep_1'=2,'rep_2'=2,'fsdp'=16] {'rep_0','rep_1'}, dimensions={0} | all-to-all | bytes 3670016 | tf_op jit(solution)/shard_map/all_to_all | solution.py:12
  243.5 1.2 copy.33
  244.7 0.5 broadcast_in_dim.13
  245.2 8.8 %all_to_all.41 = bf16[2,16,128,448]{2,1,3,0:T(8,128)(2,1)S(1)} all-to-all(bf16[2,16,128,448]{2,1,3,0:T(8,128)(2,1)S(1)} %broadcast_in_dim.13), channel_id=1, replica_groups=mesh['rep_0'=8,'rep_1'=2,'rep_2'=2,'fsdp'=16] {'rep_2'}, dimensions={0} | all-to-all | bytes 7340032 | tf_op jit(solution)/shard_map/all_to_all | solution.py:12
  254.0 7.5 %copy.34 = bf16[16,2,128,448]{2,1,0,3:T(2,128)(2,1)} copy(bf16[16,2,128,448]{2,0,3,1:T(8,128)(2,1)S(1)} %bitcast.31) | data formatting | bytes 7340032 | tf_op jit(solution)/shard_map/transpose | solution.py:26
  261.5 7.2 %reshape_reshape.11 = bf16[4096,448]{0,1:T(8,128)(2,1)} reshape(bf16[16,2,128,448]{2,1,0,3:T(2,128)(2,1)} %copy.34) | data formatting | bytes 7340032 | tf_op jit(solution)/shard_map/reshape;reshape | solution.py:20
  268.8 6.0 %fusion.9 = (f32[448]{0:T(512)S(1)}, f32[512,448]{0,1:T(8,128)S(1)}) fusion(f32[512,448]{0,1:T(8,128)S(1)} %copy-done.6, bf16[512,448]{0,1:T(8,128)(2,1)S(1)} %copy-done.3, bf16[512,448]{0,1:T(8,128)(2,1)S(1)} %copy-done.4, bf16[4096,448]{0,1:T(8,128)(2,1)} %reshape_reshape.11, bf16[512,4096]{1,0:T(8,128)(2,1)} %all-gather.2.cloned.1.call-done), kind=kOutput, calls=%fused_computation.17 | convolution fusion | flops 1883176448 | bytes 10618624 | tf_op jit(solution)/shard_map/dot_general | solution.py:100
  274.8 2.6 fusion.2
  277.5 0.7 broadcast_in_dim.14
  278.2 3.9 %all-to-all-start.6 = ((f32[32,1,896]{2,1,0:T(1,128)}), f32[32,1,896]{2,1,0:T(1,128)S(1)}, u32[]{:S(2)}, u32[]{:S(2)}) async-start(f32[32,1,896]{2,1,0:T(1,128)} %broadcast_in_dim.14), calls=%async_computation.6 | async-start | bytes 229376 | tf_op jit(solution)/shard_map/all_to_all | solution.py:12
  282.1 1.6 constant_dynamic-slice_fusion
  283.7 7.6 %all-to-all-done.6 = f32[32,1,896]{2,1,0:T(1,128)S(1)} async-done(((f32[32,1,896]{2,1,0:T(1,128)}), f32[32,1,896]{2,1,0:T(1,128)S(1)}, u32[]{:S(2)}, u32[]{:S(2)}) %all-to-all-start.6) | async-done | bytes 114720 | tf_op jit(solution)/shard_map/all_to_all | solution.py:12
  291.4 0.7 slice_multiply_fusion
  (17 shorter events, 0.2 us)
Async XLA Ops:
  7.2 105.0 %all-gather.2.cloned.1.call-start = ((), (), s32[]{:S(2)}) async-start(), calls=%async_computation.7 | async-start | bytes 4456448 | tf_op jit(solution)/shard_map/all_gather | solution.py:76
  88.0 29.8 %copy-start.3 = (bf16[512,448]{0,1:T(8,128)(2,1)S(1)}, bf16[512,448]{0,1:T(8,128)(2,1)}, u32[]{:S(2)}) copy-start(bf16[512,448]{0,1:T(8,128)(2,1)} %param.6) | copy-start | bytes 1376260
  88.0 29.8 %copy-start.4 = (bf16[512,448]{0,1:T(8,128)(2,1)S(1)}, bf16[512,448]{0,1:T(8,128)(2,1)}, u32[]{:S(2)}) copy-start(bf16[512,448]{0,1:T(8,128)(2,1)} %param.7) | copy-start | bytes 1376260
  112.2 5.6 %copy-start.1 = (bf16[512,4096]{1,0:T(8,128)(2,1)S(1)}, bf16[512,4096]{1,0:T(8,128)(2,1)}, u32[]{:S(2)}) copy-start(bf16[512,4096]{1,0:T(8,128)(2,1)} %all-gather.2.cloned.1.call-done) | copy-start | bytes 12582916
  117.8 4.1 %copy-start.5 = (f32[512,448]{0,1:T(8,128)}, f32[512,448]{0,1:T(8,128)S(1)}, u32[]{:S(2)}) copy-start(f32[512,448]{0,1:T(8,128)S(1)} %fusion.13) | copy-start | bytes 2752516
  261.5 7.2 %copy-start.6 = (f32[512,448]{0,1:T(8,128)S(1)}, f32[512,448]{0,1:T(8,128)}, u32[]{:S(2)}) copy-start(f32[512,448]{0,1:T(8,128)} %copy-done.5) | copy-start | bytes 2752516
  268.8 6.0 %copy-start = (bf16[448,4096]{1,0:T(8,128)(2,1)S(1)}, bf16[448,4096]{1,0:T(8,128)(2,1)}, u32[]{:S(2)}) copy-start(bf16[448,4096]{1,0:T(8,128)(2,1)} %convolution_convert_fusion) | copy-start | bytes 11010052
  268.8 6.1 %copy-start.2 = (bf16[512,4096]{1,0:T(8,128)(2,1)S(1)}, bf16[512,4096]{1,0:T(8,128)(2,1)}, u32[]{:S(2)}) copy-start(bf16[512,4096]{1,0:T(8,128)(2,1)} %all-gather.2.cloned.1.call-done) | copy-start | bytes 12582916
  278.2 13.1 %all-to-all-start.6 = ((f32[32,1,896]{2,1,0:T(1,128)}), f32[32,1,896]{2,1,0:T(1,128)S(1)}, u32[]{:S(2)}, u32[]{:S(2)}) async-start(f32[32,1,896]{2,1,0:T(1,128)} %broadcast_in_dim.14), calls=%async_computation.6 | async-start | bytes 229376 | tf_op jit(solution)/shard_map/all_to_all | solution.py:12
Sparse Core Ops, SparseCore 0:
  11.0 101.1 all-gather.1
where the time goes:
time: 300 us; the launch traced here: 299 us
  blocking collectives  178 us (59%)
  local copies, waits for them, and re-layouts  46.7 us (16%)
  waiting for transfers between devices  32.5 us (11%)
  matrix products  18.3 us (6%)
  between operations  14.2 us (5%)
  other arithmetic  5.04 us (2%)
  starting transfers between devices  3.92 us (1%)
    all_to_all x4, blocking collectives, copy_for_each(): lax.all_to_all(jnp.broadcast_to(value[None], (count, *value.shape)), axis...  119 us
    all_to_all x1, blocking collectives, sum_in_two_steps(): lax.all_to_all(own.astype(jnp.bfloat16), far, 0, 0, tiled=True)  51.3 us
    all_gather x1, waiting for transfers between devices, shards(): features_all = lax.all_gather(tokens, 'fsdp', axis=1, tiled=True)  24.2 us
    transpose x2, local copies, waits for them, and re-layouts, gathered_by_axis(): return in_order(blocks.swapaxes(0, 1).reshape(-1, *value.shape), dim)  15 us
    another operation x2, local copies, waits for them, and re-layouts, in_order(): blocks.reshape(*lengths[:dim], lengths[dim] * lengths[dim + 1], *lengths[...  14.4 us
    another operation x2, local copies, waits for them, and re-layouts, in_blocks(): value.reshape(*lengths[:dim], count, lengths[dim] // count, *lengths[dim...  9.59 us
    all_to_all x1, blocking collectives, summed_on_arrival(): lax.all_to_all(in_blocks(value, dim, count), axis, 0, 0, tiled=True)  7.95 us
    all_to_all x1, waiting for transfers between devices, copy_for_each(): lax.all_to_all(jnp.broadcast_to(value[None], (count, *value.shape)), axis...  7.6 us
  transfers between devices with their start and end apart: 2, of which 2 were waited for; matrix products, arithmetic and copies ran while one was open for 6% of the time, Pallas kernels for 0%

commit v1 on v0

--- a/solution.py
+++ b/solution.py
@@ -73,7 +73,9 @@
 
 
 def shards(tokens, gate_weight, up_act, cotangent):
-    features_all = lax.all_gather(tokens, "fsdp", axis=1, tiled=True)
+    features_all = jnp.concatenate(
+        lax.all_to_all(jnp.stack([tokens] * lax.axis_size("fsdp")), "fsdp", 0, 0), axis=1
+    )
     replicas = lax.axis_size(REP)
     gate_pre = jnp.dot(
         features_all,

time: 300 us -> 367 us (1.22)
  waiting for transfers between devices: 32.5 us -> 132 us
  blocking collectives: 178 us -> 127 us
  starting transfers between devices: 3.92 us -> 25.2 us
  between operations: 14.2 us -> 0.78 us
  local copies, waits for them, and re-layouts: 46.7 us -> 52.5 us
  matrix products: 18.3 us -> 22.8 us
    all_to_all x0 -> x1, waiting for transfers between devices: none -> 83 us  [shards(): lax.all_to_all(jnp.stack([tokens] * lax.axis_size('fsdp')), 'fsdp', 0, 0)]
    all_to_all x4 -> x3, blocking collectives: 119 us -> 68 us  [copy_for_each(): lax.all_to_all(jnp.broadcast_to(value[None], (count, *value.shape)), axis...]
    all_to_all x1 -> x2, waiting for transfers between devices: 7.6 us -> 49.4 us  [copy_for_each(): lax.all_to_all(jnp.broadcast_to(value[None], (count, *value.shape)), axis...]
    all_gather x1 -> x0, waiting for transfers between devices: 24.2 us -> none  [shards(): features_all = lax.all_gather(tokens, 'fsdp', axis=1, tiled=True)]
    all_to_all x0 -> x1, starting transfers between devices: none -> 11.8 us  [shards(): lax.all_to_all(jnp.stack([tokens] * lax.axis_size('fsdp')), 'fsdp', 0, 0)]
    all_to_all x1 -> x2, starting transfers between devices: 3.88 us -> 13.4 us  [copy_for_each(): lax.all_to_all(jnp.broadcast_to(value[None], (count, *value.shape)), axis...]
  transfers between devices with their start and end apart: 2 -> 3, of which waited for: 2 -> 3; matrix products, arithmetic and copies ran while one was open for 6% -> 5% of each run, Pallas kernels for 0% -> 0%
where the time goes in v1:
time: 367 us; the launch traced here: 366 us
  waiting for transfers between devices  132 us (36%)
  blocking collectives  127 us (35%)
  local copies, waits for them, and re-layouts  52.5 us (14%)
  starting transfers between devices  25.2 us (7%)
  matrix products  22.8 us (6%)
  other arithmetic  5.04 us (1%)
    all_to_all x1, waiting for transfers between devices, shards(): lax.all_to_all(jnp.stack([tokens] * lax.axis_size('fsdp')), 'fsdp', 0, 0)  83 us
    all_to_all x3, blocking collectives, copy_for_each(): lax.all_to_all(jnp.broadcast_to(value[None], (count, *value.shape)), axis...  68 us
    all_to_all x2, waiting for transfers between devices, copy_for_each(): lax.all_to_all(jnp.broadcast_to(value[None], (count, *value.shape)), axis...  49.4 us
    all_to_all x1, blocking collectives, sum_in_two_steps(): lax.all_to_all(own.astype(jnp.bfloat16), far, 0, 0, tiled=True)  49 us
    transpose x2, local copies, waits for them, and re-layouts, gathered_by_axis(): return in_order(blocks.swapaxes(0, 1).reshape(-1, *value.shape), dim)  17.1 us
    another operation x2, local copies, waits for them, and re-layouts, in_order(): blocks.reshape(*lengths[:dim], lengths[dim] * lengths[dim + 1], *lengths[...  14.4 us
    all_to_all x2, starting transfers between devices, copy_for_each(): lax.all_to_all(jnp.broadcast_to(value[None], (count, *value.shape)), axis...  13.4 us
    all_to_all x1, starting transfers between devices, shards(): lax.all_to_all(jnp.stack([tokens] * lax.axis_size('fsdp')), 'fsdp', 0, 0)  11.8 us
  transfers between devices with their start and end apart: 3, of which 3 were waited for; matrix products, arithmetic and copies ran while one was open for 5% of the time, Pallas kernels for 0%

profile of v1, /device:TPU:1, one launch (start us, length us, event | category | flops | bytes accessed | tf_op | source)
XLA Modules:
  0.0 365.8 jit_solution(12062016937001300600)
XLA Ops:
  0.6 2.5 broadcast_in_dim.10
  3.2 9.6 %all-to-all-start.1 = ((bf16[16,128,448]{1,2,0:T(8,128)(2,1)}), bf16[16,128,448]{1,2,0:T(8,128)(2,1)S(1)}, u32[]{:S(2)}, u32[]{:S(2)}) async-start(bf16[16,128,448]{1,2,0:T(8,128)(2,1)} %broadcast_in_dim.10), calls=%async_computation.1 | async-start | bytes 3670016 | tf_op jit(solution)/shard_map/all_to_all | solution.py:12
  12.9 41.8 %all-to-all-done.1 = bf16[16,128,448]{1,2,0:T(8,128)(2,1)S(1)} async-done(((bf16[16,128,448]{1,2,0:T(8,128)(2,1)}), bf16[16,128,448]{1,2,0:T(8,128)(2,1)S(1)}, u32[]{:S(2)}, u32[]{:S(2)}) %all-to-all-start.1) | async-done | bytes 1835040 | tf_op jit(solution)/shard_map/all_to_all | solution.py:12
  54.7 1.2 copy.33
  55.9 0.5 broadcast_in_dim.11
  56.4 11.5 %all_to_all.41 = bf16[2,16,128,448]{2,1,3,0:T(8,128)(2,1)} all-to-all(bf16[2,16,128,448]{2,1,3,0:T(8,128)(2,1)S(1)} %broadcast_in_dim.11), channel_id=1, replica_groups=mesh['rep_0'=8,'rep_1'=2,'rep_2'=2,'fsdp'=16] {'rep_2'}, dimensions={0} | all-to-all | bytes 7340032 | tf_op jit(solution)/shard_map/all_to_all | solution.py:12
  67.8 2.4 stack.2
  70.2 11.8 %all-to-all-start = ((bf16[16,512,256]{1,2,0:T(8,128)(2,1)}), bf16[16,512,256]{1,2,0:T(8,128)(2,1)}, u32[]{:S(2)}, u32[]{:S(2)}) async-start(bf16[16,512,256]{1,2,0:T(8,128)(2,1)} %stack.2), calls=%async_computation | async-start | bytes 8388608 | tf_op jit(solution)/shard_map/all_to_all | solution.py:77
  82.0 9.5 %copy.34 = bf16[16,2,128,448]{2,1,0,3:T(2,128)(2,1)} copy(bf16[16,2,128,448]{2,0,3,1:T(8,128)(2,1)} %bitcast.32) | data formatting | bytes 7340032 | tf_op jit(solution)/shard_map/transpose | solution.py:26
  91.5 7.1 %reshape_reshape.9 = bf16[4096,448]{0,1:T(8,128)(2,1)} reshape(bf16[16,2,128,448]{2,1,0,3:T(2,128)(2,1)} %copy.34) | data formatting | bytes 7340032 | tf_op jit(solution)/shard_map/reshape;reshape | solution.py:20
  98.6 83.0 %all-to-all-done = bf16[16,512,256]{1,2,0:T(8,128)(2,1)} async-done(((bf16[16,512,256]{1,2,0:T(8,128)(2,1)}), bf16[16,512,256]{1,2,0:T(8,128)(2,1)}, u32[]{:S(2)}, u32[]{:S(2)}) %all-to-all-start) | async-done | bytes 4194336 | tf_op jit(solution)/shard_map/all_to_all | solution.py:77
  181.6 5.4 %fusion.13 = f32[512,448]{0,1:T(8,128)S(1)} fusion(bf16[4096,448]{0,1:T(8,128)(2,1)} %reshape_reshape.9, bf16[512,4096]{0,1:T(8,128)(2,1)} %bitcast.1), kind=kOutput, calls=%fused_computation.25 | convolution fusion | flops 1879048192 | bytes 8781824 | tf_op jit(solution)/shard_map/dot_general | solution.py:80
  187.1 6.6 %convolution_convert_fusion = bf16[448,4096]{1,0:T(8,128)(2,1)} fusion(bf16[512,4096]{0,1:T(8,128)(2,1)} %bitcast.1, f32[512,448]{0,1:T(8,128)S(1)} %fusion.13, bf16[512,448]{0,1:T(8,128)(2,1)S(1)} %copy-done.2, bf16[512,448]{0,1:T(8,128)(2,1)S(1)} %copy-done.3), kind=kOutput, calls=%fused_computation | convolution fusion | flops 1883635712 | bytes 9699328 | tf_op jit(solution)/shard_map/dot_general | solution.py:91
  193.7 7.1 %reshape_reshape.10 = bf16[16,2,128,448]{2,1,0,3:T(2,128)(2,1)} reshape(bf16[4096,448]{0,1:T(8,128)(2,1)} %bitcast.35) | data formatting | bytes 7340032 | tf_op jit(solution)/shard_map/reshape;reshape | solution.py:36
  200.8 2.5 copy.46
  203.3 10.0 %all_to_all.42 = bf16[2,16,128,448]{2,1,3,0:T(8,128)(2,1)} all-to-all(bf16[2,16,128,448]{2,1,3,0:T(8,128)(2,1)S(1)} %bitcast.33), channel_id=1, replica_groups=mesh['rep_0'=8,'rep_1'=2,'rep_2'=2,'fsdp'=16] {'rep_2'}, dimensions={0} | all-to-all | bytes 7340032 | tf_op jit(solution)/shard_map/all_to_all | solution.py:42
  213.4 4.0 %reduce_sum.51 = bf16[16,128,448]{1,0,2:T(8,128)(2,1)S(1)} reduce(bf16[2,16,128,448]{2,1,3,0:T(8,128)(2,1)} %all_to_all.42, bf16[]{:T(256)} %constant.11.clone.1), dimensions={0}, to_apply=%region_0.1 | reduce | flops 917504 | bytes 5505026 | tf_op jit(solution)/shard_map/reduce_sum | solution.py:43
  217.3 0.5 copy.37
  217.8 49.0 %all_to_all.43 = bf16[16,128,448]{1,2,0:T(8,128)(2,1)S(1)} all-to-all(bf16[16,128,448]{1,2,0:T(8,128)(2,1)S(1)} %copy.37), channel_id=1, replica_groups=mesh['rep_0'=8,'rep_1'=2,'rep_2'=2,'fsdp'=16] {'rep_0','rep_1'}, dimensions={0} | all-to-all | bytes 3670016 | tf_op jit(solution)/shard_map/all_to_all | solution.py:50
  267.5 47.7 %all_to_all.44 = bf16[16,128,448]{1,2,0:T(8,128)(2,1)S(1)} all-to-all(bf16[16,128,448]{1,2,0:T(8,128)(2,1)S(1)} %broadcast_in_dim.12), channel_id=1, replica_groups=mesh['rep_0'=8,'rep_1'=2,'rep_2'=2,'fsdp'=16] {'rep_0','rep_1'}, dimensions={0} | all-to-all | bytes 3670016 | tf_op jit(solution)/shard_map/all_to_all | solution.py:12
  315.2 1.2 copy.38
  316.4 0.5 broadcast_in_dim.13
  316.9 8.8 %all_to_all.45 = bf16[2,16,128,448]{2,1,3,0:T(8,128)(2,1)S(1)} all-to-all(bf16[2,16,128,448]{2,1,3,0:T(8,128)(2,1)S(1)} %broadcast_in_dim.13), channel_id=1, replica_groups=mesh['rep_0'=8,'rep_1'=2,'rep_2'=2,'fsdp'=16] {'rep_2'}, dimensions={0} | all-to-all | bytes 7340032 | tf_op jit(solution)/shard_map/all_to_all | solution.py:12
  325.6 7.5 %copy.39 = bf16[16,2,128,448]{2,1,0,3:T(2,128)(2,1)} copy(bf16[16,2,128,448]{2,0,3,1:T(8,128)(2,1)S(1)} %bitcast.34) | data formatting | bytes 7340032 | tf_op jit(solution)/shard_map/transpose | solution.py:26
  333.2 7.2 %reshape_reshape.11 = bf16[4096,448]{0,1:T(8,128)(2,1)} reshape(bf16[16,2,128,448]{2,1,0,3:T(2,128)(2,1)} %copy.39) | data formatting | bytes 7340032 | tf_op jit(solution)/shard_map/reshape;reshape | solution.py:20
  340.4 6.0 %fusion.9 = (f32[448]{0:T(512)S(1)}, f32[512,448]{0,1:T(8,128)S(1)}) fusion(f32[512,448]{0,1:T(8,128)S(1)} %copy-done.5, bf16[512,448]{0,1:T(8,128)(2,1)S(1)} %copy-done.2, bf16[512,448]{0,1:T(8,128)(2,1)S(1)} %copy-done.3, bf16[4096,448]{0,1:T(8,128)(2,1)} %reshape_reshape.11, bf16[512,4096]{0,1:T(8,128)(2,1)} %bitcast.1), kind=kOutput, calls=%fused_computation.17 | convolution fusion | flops 1883176448 | bytes 10618624 | tf_op jit(solution)/shard_map/dot_general | solution.py:102
  346.4 4.8 %fusion.2 = f32[448]{0:T(512)S(1)} fusion(f32[512,448]{0,1:T(8,128)S(1)} %get-tuple-element.6, bf16[448,4096]{1,0:T(8,128)(2,1)S(1)} %copy-done, bf16[512,4096]{0,1:T(8,128)(2,1)} %bitcast.1, f32[512,448]{0,1:T(8,128)S(1)} %copy-done.5, bf16[512,448]{0,1:T(8,128)(2,1)S(1)} %copy-done.2, bf16[512,448]{0,1:T(8,128)(2,1)S(1)} %copy-done.3), kind=kOutput, calls=%fused_computation.10 | convolution fusion | flops 1883176448 | bytes 10618624 | tf_op jit(solution)/shard_map/dot_general | solution.py:94
  351.3 0.7 broadcast_in_dim.14
  352.0 3.9 %all-to-all-start.7 = ((f32[32,1,896]{2,1,0:T(1,128)}), f32[32,1,896]{2,1,0:T(1,128)S(1)}, u32[]{:S(2)}, u32[]{:S(2)}) async-start(f32[32,1,896]{2,1,0:T(1,128)} %broadcast_in_dim.14), calls=%async_computation.7 | async-start | bytes 229376 | tf_op jit(solution)/shard_map/all_to_all | solution.py:12
  355.9 1.6 constant_dynamic-slice_fusion
  357.4 7.6 %all-to-all-done.7 = f32[32,1,896]{2,1,0:T(1,128)S(1)} async-done(((f32[32,1,896]{2,1,0:T(1,128)}), f32[32,1,896]{2,1,0:T(1,128)S(1)}, u32[]{:S(2)}, u32[]{:S(2)}) %all-to-all-start.7) | async-done | bytes 114720 | tf_op jit(solution)/shard_map/all_to_all | solution.py:12
  365.1 0.7 slice_multiply_fusion
  (17 shorter events, 0.9 us)
Async XLA Ops:
  0.6 12.1 %copy-start.1 = (bf16[512,256]{1,0:T(8,128)(2,1)S(1)}, bf16[512,256]{1,0:T(8,128)(2,1)}, u32[]{:S(2)}) copy-start(bf16[512,256]{1,0:T(8,128)(2,1)} %param.4) | copy-start | bytes 786436
  3.2 51.5 %all-to-all-start.1 = ((bf16[16,128,448]{1,2,0:T(8,128)(2,1)}), bf16[16,128,448]{1,2,0:T(8,128)(2,1)S(1)}, u32[]{:S(2)}, u32[]{:S(2)}) async-start(bf16[16,128,448]{1,2,0:T(8,128)(2,1)} %broadcast_in_dim.10), calls=%async_computation.1 | async-start | bytes 3670016 | tf_op jit(solution)/shard_map/all_to_all | solution.py:12
  70.2 111.4 %all-to-all-start = ((bf16[16,512,256]{1,2,0:T(8,128)(2,1)}), bf16[16,512,256]{1,2,0:T(8,128)(2,1)}, u32[]{:S(2)}, u32[]{:S(2)}) async-start(bf16[16,512,256]{1,2,0:T(8,128)(2,1)} %stack.2), calls=%async_computation | async-start | bytes 8388608 | tf_op jit(solution)/shard_map/all_to_all | solution.py:77
  181.6 5.4 %copy-start.2 = (bf16[512,448]{0,1:T(8,128)(2,1)S(1)}, bf16[512,448]{0,1:T(8,128)(2,1)}, u32[]{:S(2)}) copy-start(bf16[512,448]{0,1:T(8,128)(2,1)} %param.6) | copy-start | bytes 1376260
  181.6 5.4 %copy-start.3 = (bf16[512,448]{0,1:T(8,128)(2,1)S(1)}, bf16[512,448]{0,1:T(8,128)(2,1)}, u32[]{:S(2)}) copy-start(bf16[512,448]{0,1:T(8,128)(2,1)} %param.7) | copy-start | bytes 1376260
  187.1 6.7 %copy-start.4 = (f32[512,448]{0,1:T(8,128)}, f32[512,448]{0,1:T(8,128)S(1)}, u32[]{:S(2)}) copy-start(f32[512,448]{0,1:T(8,128)S(1)} %fusion.13) | copy-start | bytes 2752516
  333.2 7.2 %copy-start.5 = (f32[512,448]{0,1:T(8,128)S(1)}, f32[512,448]{0,1:T(8,128)}, u32[]{:S(2)}) copy-start(f32[512,448]{0,1:T(8,128)} %copy-done.4) | copy-start | bytes 2752516
  340.4 6.0 %copy-start = (bf16[448,4096]{1,0:T(8,128)(2,1)S(1)}, bf16[448,4096]{1,0:T(8,128)(2,1)}, u32[]{:S(2)}) copy-start(bf16[448,4096]{1,0:T(8,128)(2,1)} %convolution_convert_fusion) | copy-start | bytes 11010052
  352.0 13.1 %all-to-all-start.7 = ((f32[32,1,896]{2,1,0:T(1,128)}), f32[32,1,896]{2,1,0:T(1,128)S(1)}, u32[]{:S(2)}, u32[]{:S(2)}) async-start(f32[32,1,896]{2,1,0:T(1,128)} %broadcast_in_dim.14), calls=%async_computation.7 | async-start | bytes 229376 | tf_op jit(solution)/shard_map/all_to_all | solution.py:12
